TPU v7x, 128 devices: a whole 4x4x4 slice. The times are simulated.
128 devices in a mesh: centers: 32 (over y, z_hi, x), nys: 4 (over z_lo, core).
Axes of the slice: x: 4, y: 4, z: 4 (z_hi: 2, z_lo: 2; z = z_hi * 2 + z_lo), core: 2. Of those that a mesh axis runs over, the one named last changes fastest.
Arguments:
- centers: bfloat16 [262144, 1024], P(('centers', 'nys'))
- weights: bfloat16 [262144, 1000], P(('centers', 'nys')), may hold values from -1.5 to 1.5
- labels: bfloat16 [262144, 1000], P(('centers', 'nys')), may hold values from -6 to 6
- loader: int32 [1], replicated, may hold values from 0 to 127
- sample_ids: int32 [1024], replicated, may hold values from 0 to 2047, as said below
- nys_ids: int32 [16384], P(('centers', 'nys')), may hold values from 0 to 2047, as said below
- eigen_vectors: bfloat16 [16384, 160], P('centers', 'nys'), may hold values from -0.046875 to 0.046875
- eigen_scale: float32 [160], replicated, may hold values from 2 to 40
Outputs:
- new_weights: bfloat16 [262144, 1000], P(('centers', 'nys'))
- residual: bfloat16 [1024, 1000], replicated
Inputs may be any that keep to these rules, and one draw needn't show every extreme that they name: `sample_ids`: each entry is a row of the loader's block of 2048 centers; repeats may occur. `nys_ids`: entry j is a row of the block of 2048 centers with the same block index as row j of the subsample; repeats may occur.
All inputs are finite; a program needn't handle non-finite values.
Results may differ from a plain program's by a relative error of at most 0.0095.
Values may be sent and summed in bfloat16 or wider, within the bound.
A program may use at most 128 MiB of HBM per device.

v0:
```python
import jax
import jax.numpy as jnp
from jax import lax
from jax.sharding import PartitionSpec as P

learn_rate = 0.5
kernel_width = 0.25


def from_root(value, axis, source):
    kept = jnp.where(lax.axis_index(axis) == source, value, 0).astype(value.dtype)
    return lax.psum(kept, axis)


def kernel(left_rows, right_rows):
    left_sq = jnp.sum(jnp.square(left_rows.astype(jnp.float32)), axis=1)
    right_sq = jnp.sum(jnp.square(right_rows.astype(jnp.float32)), axis=1)
    inner_prod = lax.dot_general(
        left_rows, right_rows, (((1,), (1,)), ((), ())), preferred_element_type=jnp.float32
    )
    distance = jnp.sqrt(jnp.maximum(left_sq[:, None] + right_sq[None, :] - 2.0 * inner_prod, 0.0))
    return jnp.exp(-distance / kernel_width).astype(jnp.bfloat16)


def body(centers, weights, labels, loader, sample_ids, nys_ids, eigen_vectors, eigen_scale):
    loader_dev = loader[0]
    is_owner = lax.axis_index(("centers", "nys")) == loader_dev
    sub_count = nys_ids.shape[0]
    eigen_block = lax.all_gather(eigen_vectors, "nys", axis=1, tiled=True)
    own_vectors = lax.dynamic_slice_in_dim(
        eigen_block, lax.axis_index("nys") * sub_count, sub_count, 0
    )
    picked = jnp.take(centers, sample_ids, axis=0)
    targets = jnp.take(labels, sample_ids, axis=0).astype(jnp.float32)
    target_term = jnp.where(is_owner, targets, 0.0)
    minibatch = from_root(picked, ("centers", "nys"), loader_dev)
    kernel_rows = kernel(minibatch, centers)
    predicted = jnp.dot(kernel_rows, weights, preferred_element_type=jnp.float32)
    summed_rows = lax.psum(predicted - target_term, ("centers", "nys"))
    residual = summed_rows.astype(jnp.bfloat16)
    subsample = jnp.take(centers, nys_ids, axis=0)
    kernel_sub = kernel(subsample, minibatch)
    projected = jnp.dot(kernel_sub, residual, preferred_element_type=jnp.float32).astype(
        jnp.bfloat16
    )
    local_coef = lax.dot_general(
        own_vectors, projected, (((0,), (0,)), ((), ())), preferred_element_type=jnp.float32
    )
    reduced = lax.psum(local_coef, ("centers", "nys"))
    coefficients = (eigen_scale[:, None] * reduced).astype(jnp.bfloat16)
    correction = jnp.dot(own_vectors, coefficients, preferred_element_type=jnp.float32)
    weight_step = jnp.zeros(weights.shape, jnp.float32).at[nys_ids].add(learn_rate * correction)
    batch_scale = jnp.where(is_owner, -learn_rate, 0.0)
    weight_step = weight_step.at[sample_ids].add(batch_scale * residual.astype(jnp.float32))
    new_weights = (weights.astype(jnp.float32) + weight_step).astype(jnp.bfloat16)
    return (new_weights, residual)


def solution(mesh):
    placed = (
        P(("centers", "nys"), None),
        P(("centers", "nys"), None),
        P(("centers", "nys"), None),
        P(),
        P(),
        P(("centers", "nys")),
        P("centers", "nys"),
        P(),
    )
    return jax.shard_map(
        body,
        mesh=mesh,
        in_specs=placed,
        out_specs=(P(("centers", "nys"), None), P()),
        check_vma=False,
    )
```

profile of v0, /device:TPU:1, one launch (start us, length us, event | category | flops | bytes accessed | tf_op | source)
XLA Modules:
  0.0 487.4 jit_solution(1329588900002197232)
XLA Ops:
  7.2 0.0 all-reduce.4.cloned.1.call-start
  7.2 0.7 compare_select_fusion
  7.9 0.7 compare_and_fusion
  9.3 7.7 %gather_fusion.1 = bf16[1024,1024]{1,0:T(8,128)(2,1)S(1)} fusion(bf16[2048,1024]{1,0:T(8,128)(2,1)} %param.8, s32[1024]{0:T(1024)S(1)} %get-tuple-element.7), kind=kCustom, calls=%fused_computation.1 | custom fusion | bytes 4198400 | tf_op jit(solution)/shard_map/jit(_take)/gather | solution.py:33
  17.0 1.6 select_select_fusion
  18.6 0.0 all-reduce.4.cloned.1.call-update
  18.6 0.0 all-reduce.6.cloned.1.call-start
  18.7 6.4 %copy.18 = bf16[2048,1000]{1,0:T(8,128)(2,1)} copy(bf16[2048,1000]{0,1:T(8,128)(2,1)} %param.10) | data formatting | bytes 8192000 | tf_op args[2]
  25.1 7.7 %gather_fusion.2 = bf16[1024,1000]{1,0:T(8,128)(2,1)S(1)} fusion(bf16[2048,1000]{1,0:T(8,128)(2,1)} %copy.18, s32[1024]{0:T(1024)S(1)} %get-tuple-element.7), kind=kCustom, calls=%fused_computation.2 | custom fusion | bytes 4100096 | tf_op jit(solution)/shard_map/jit(_take)/gather | solution.py:34
  32.8 0.0 copy-start.4
  32.8 2.4 copy.19
  35.2 3.8 gather_fusion
  39.0 6.9 %copy.20 = f32[2048,1000]{1,0:T(8,128)} copy(bf16[2048,1000]{0,1:T(8,128)(2,1)} %param.9) | data formatting | bytes 12288000 | tf_op jit(solution)/shard_map/convert_element_type | solution.py:55
  45.9 7.6 %all_gather.3 = bf16[512,160]{0,1:T(8,128)(2,1)S(1)} all-gather(bf16[512,40]{0,1:T(8,128)(2,1)S(1)} %copy-done.2), channel_id=1, replica_groups=mesh['centers'=32,'nys'=4] {'nys'}, dimensions={1}, use_global_device_ids=true | all-gather | bytes 204800 | tf_op jit(solution)/shard_map/all_gather | solution.py:29
  53.5 0.2 multiply_reduce_fusion.2
  53.7 3.1 multiply_reduce_fusion
  56.9 115.5 %all-reduce.4.cloned.1.call-done = bf16[1024,1024]{1,0:T(8,128)(2,1)} async-done(((bf16[1024,1024]{1,0:T(8,128)(2,1)}), bf16[1024,1024]{1,0:T(8,128)(2,1)}) %all-reduce.4.cloned.1.call-update) | async-done | bytes 2097168 | tf_op jit(solution)/shard_map/psum | solution.py:12
  172.3 2.1 multiply_reduce_fusion.1
  174.4 15.2 %select_subtract_fusion = f32[1024,1000]{0,1:T(8,128)} fusion(bf16[1024,1000]{0,1:T(8,128)(2,1)S(1)} %copy-done.1, pred[1024]{0:T(1024)(128)(4,1)S(1)} %compare_and_fusion, pred[]{:T(512)S(6)} %eq.4, bf16[2048,1000]{0,1:T(8,128)(2,1)} %param.9, bf16[1024,1024]{1,0:T(8,128)(2,1)} %all-reduce.4.cloned.1.call-done, bf16[2048,1024]{1,0:T(8,128)(2,1)} %param.8, ...), kind=kOutput, calls=%fused_computation.9 | convolution fusion | flops 8508047360 | bytes 16544769 | tf_op jit(solution)/shard_map/dot_general | solution.py:38
  189.6 102.9 %all-reduce.7 = bf16[1024,1000]{0,1:T(8,128)(2,1)S(1)} all-reduce(f32[1024,1000]{0,1:T(8,128)} %select_subtract_fusion), channel_id=1, replica_groups=mesh['centers'=32,'nys'=4] {'centers','nys'}, use_global_device_ids=true, to_apply=%region_4.5 | all-reduce | flops 1024000 | bytes 6144000 | tf_op jit(solution)/shard_map/psum | solution.py:39
  292.6 4.0 convolution_convert_fusion
  296.5 1.1 fusion.15
  297.7 0.0 all-reduce.6.cloned.1.call-update
  297.7 2.6 convert_multiply_fusion
  300.3 5.3 %copy.22 = f32[1024,1000]{1,0:T(8,128)} copy(f32[1024,1000]{0,1:T(8,128)} %convert_multiply_fusion) | data formatting | bytes 8192000 | tf_op jit(solution)/shard_map/mul | solution.py:54
  305.6 135.6 %all-reduce.6.cloned.1.call-done = f32[160,1000]{1,0:T(8,128)} async-done(((f32[160,1000]{1,0:T(8,128)}), f32[160,1000]{1,0:T(8,128)}) %all-reduce.6.cloned.1.call-update) | async-done | bytes 640016 | tf_op jit(solution)/shard_map/psum | solution.py:49
  441.2 1.6 convolution_multiply_fusion.1
  442.8 0.2 copy.21
  443.0 8.2 %scatter_fusion = f32[2048,1000]{1,0:T(8,128)} fusion(f32[2048,1000]{1,0:T(8,128)} %copy.20, s32[128]{0:T(128)S(1)} %compare_select_fusion.1, f32[128,1000]{1,0:T(8,128)S(1)} %copy.21), kind=kCustom, calls=%fused_computation.3 | custom fusion | flops 128000 | bytes 1536512 | tf_op jit(solution)/shard_map/scatter-add | solution.py:52
  451.2 16.9 %scatter_fusion.1 = f32[2048,1000]{1,0:T(8,128)} fusion(f32[2048,1000]{1,0:T(8,128)} %scatter_fusion, s32[1024]{0:T(1024)S(1)} %get-tuple-element.6, f32[1024,1000]{1,0:T(8,128)} %copy.22), kind=kCustom, calls=%fused_computation.4 | custom fusion | flops 1024000 | bytes 12292096 | tf_op jit(solution)/shard_map/scatter-add | solution.py:54
  468.0 6.0 %convert_element_type.50 = bf16[2048,1000]{1,0:T(8,128)(2,1)} convert(f32[2048,1000]{1,0:T(8,128)} %scatter_fusion.1) | non-fusion elementwise | flops 2048000 | bytes 12288000 | tf_op jit(solution)/shard_map/convert_element_type | solution.py:55
  474.1 6.5 %copy.23 = bf16[2048,1000]{0,1:T(8,128)(2,1)} copy(bf16[2048,1000]{1,0:T(8,128)(2,1)} %convert_element_type.50) | data formatting | bytes 8192000
  (12 shorter events, 0.0 us)
Async XLA Ops:
  7.2 165.2 %all-reduce.4.cloned.1.call-start = ((), (), s32[]{:S(2)}) async-start(), calls=%async_computation | async-start | bytes 4194304 | tf_op jit(solution)/shard_map/psum | solution.py:12
  18.6 422.6 %all-reduce.6.cloned.1.call-start = ((), (), s32[]{:S(2)}) async-start(), calls=%async_computation.1 | async-start | bytes 1310720 | tf_op jit(solution)/shard_map/psum | solution.py:49
  32.8 2.4 copy-start.4
  39.0 6.9 %copy-start.2 = (bf16[512,40]{0,1:T(8,128)(2,1)S(1)}, bf16[512,40]{0,1:T(8,128)(2,1)}, u32[]{:S(2)}) copy-start(bf16[512,40]{0,1:T(8,128)(2,1)} %param.14) | copy-start | bytes 122884
  45.9 128.5 %copy-start.1 = (bf16[1024,1000]{0,1:T(8,128)(2,1)S(1)}, bf16[1024,1000]{0,1:T(8,128)(2,1)}, u32[]{:S(2)}) copy-start(bf16[1024,1000]{0,1:T(8,128)(2,1)} %copy.19) | copy-start | bytes 6144004
  292.5 7.7 %copy-start = (bf16[1024,1000]{0,1:T(8,128)(2,1)}, bf16[1024,1000]{0,1:T(8,128)(2,1)S(1)}, u32[]{:S(2)}) copy-start(bf16[1024,1000]{0,1:T(8,128)(2,1)S(1)} %all-reduce.7) | copy-start | bytes 6144004
  300.3 141.0 %copy-start.3 = (f32[160]{0:T(256)S(1)}, f32[160]{0:T(256)}, u32[]{:S(2)}) copy-start(f32[160]{0:T(256)} %param.15) | copy-start | bytes 1924
Sparse Core Ops, SparseCore 0:
  18.7 153.5 all-reduce.3
  297.8 143.3 all-reduce.5
where the time goes:
time: 489 us; the launch traced here: 487 us
  waiting for transfers between devices  251 us (51%)
  blocking collectives  110 us (22%)
  local copies, waits for them, and re-layouts  46.9 us (10%)
  other arithmetic  42.1 us (9%)
  matrix products  21.9 us (4%)
  between operations  14.8 us (3%)
    psum x1, waiting for transfers between devices, body(): reduced = lax.psum(local_coef, ('centers', 'nys'))  136 us
    psum x1, waiting for transfers between devices, from_root(): return lax.psum(kept, axis)  115 us
    psum x1, blocking collectives, body(): summed_rows = lax.psum(predicted - target_term, ('centers', 'nys'))  103 us
    scatter-add x1, other arithmetic, body(): weight_step.at[sample_ids].add(batch_scale * residual.astype(jnp.float32))  16.9 us
    dot_general x1, matrix products, body(): jnp.dot(kernel_rows, weights, preferred_element_type=jnp.float32)  15.2 us
    unnamed x12, local copies, waits for them, and re-layouts  12.9 us
    gather x2, local copies, waits for them, and re-layouts, body(): targets = jnp.take(labels, sample_ids, axis=0).astype(jnp.float32)  10.1 us
  transfers between devices with their start and end apart: 2, of which 2 were waited for; matrix products, arithmetic and copies ran while one was open for 8% of the time, Pallas kernels for 0%

commit v1 on v0

v1 whole, which is shorter than its diff:
```python
import jax
import jax.numpy as jnp
from jax import lax
from jax.experimental import pallas as pl
from jax.experimental.pallas import tpu as pltpu
from jax.sharding import PartitionSpec as P

MESH = pl.DeviceIdType.MESH
BF16, F32 = jnp.bfloat16, jnp.float32

learn_rate = 0.5
kernel_width = 0.25

D, OUT, Q, BATCH, C_DEV, NYS_DEV = 1024, 1000, 160, 1024, 2048, 128
HALF = BATCH // 2
ROWS = 1280
EIG_ROW = 1008
BCAST_PARTS = (((0, 16), (0, 1, 2)), ((16, 16), (1, 2, 0)))
SUM_PARTS = (((0, 32), (0, 1, 2)), ((32, 32), (1, 2, 0)), ((64, 16), (2, 0, 1)))
NT = (((1,), (1,)), ((), ()))


def position():
    c, n = lax.axis_index("centers"), lax.axis_index("nys")
    x, y = lax.rem(c, 4), lax.div(c, 8)
    z = lax.rem(lax.div(c, 4), 2) * 2 + lax.div(n, 2)
    return (x, y, z), lax.rem(n, 2)


def device(chip, core):
    x, y, z = chip
    return ((y * 2 + lax.div(z, 2)) * 4 + x, lax.rem(z, 2) * 2 + core)


def peer_at(chip, core, axis, step):
    moved = list(chip)
    moved[axis] = lax.rem(chip[axis] + step, 4)
    return tuple(moved), device(moved, core)


def span(fixed, axis):
    return pl.ds(fixed[axis], 1) if axis in fixed else pl.ds(0, 4)


def bcast_index(core, part, fixed):
    (first, count), _ = part
    columns = pl.ds(pl.multiple_of(fixed[2] * 256, 256), 256) if 2 in fixed else pl.ds(0, D)
    return (pl.ds(core, 1), span(fixed, 0), span(fixed, 1), pl.ds(first, count), columns)


def sum_index(core, part, fixed):
    (first, count), _ = part
    if 2 in fixed:
        columns = pl.ds(pl.multiple_of(core * HALF + fixed[2] * 128, 128), 128)
    else:
        columns = pl.ds(pl.multiple_of(core * HALF, HALF), HALF)
    return (span(fixed, 0), span(fixed, 1), pl.ds(first, count), columns)


def bcast_shape(part, axes):
    (_, count), _ = part
    return (1, 1 if 0 in axes else 4, 1 if 1 in axes else 4, count, 256 if 2 in axes else D)


def sum_shape(part, axes):
    (_, count), _ = part
    return (1 if 0 in axes else 4, 1 if 1 in axes else 4, count, 128 if 2 in axes else HALF)


class Links:
    def __init__(self, send_sems, recv_sems):
        self.send_sems, self.recv_sems, self.copies = send_sems, recv_sems, []

    def start(self, source, target, to):
        i = len(self.copies)
        copy = pltpu.make_async_remote_copy(
            src_ref=source, dst_ref=target, send_sem=self.send_sems.at[i], recv_sem=self.recv_sems.at[i],
            device_id=to, device_id_type=MESH,
        )
        copy.start()
        self.copies.append(copy)
        return copy

    def wait_sends(self):
        for copy in self.copies:
            copy.wait_send()


def scatter_start(links, buffer, slots, index, chip, core, part, stage):
    axes = part[1]
    fixed = {a: chip[a] for a in axes[:stage]}
    out = []
    for step in (2, 1, 3):
        moved, to = peer_at(chip, core, axes[stage], step)
        share = {**fixed, axes[stage]: moved[axes[stage]]}
        out.append(links.start(buffer.at[index(core, part, share)], slots.at[step - 1], to))
    return out


def scatter_finish(copies, buffer, slots, index, chip, core, part, stage, result):
    for copy in copies:
        copy.wait_recv()
    own = index(core, part, {a: chip[a] for a in part[1][: stage + 1]})
    total = buffer[own].astype(F32)
    for step in range(3):
        total += slots[step].astype(F32)
    result[own] = total.astype(BF16)


def gather_start(links, buffer, index, chip, core, part, stage):
    axes = part[1]
    own = index(core, part, {a: chip[a] for a in axes[: stage + 1]})
    return [
        links.start(buffer.at[own], buffer.at[own], peer_at(chip, core, axes[stage], step)[1]) for step in (2, 1, 3)
    ]


def step_kernel(
    loader_ref, ids_ref, nys_ref, eig_ref, centers_hbm, weights_hbm, labels_hbm,
    sums_hbm, pick_hbm, spread_hbm,
    cent, wts, labs, pick, stack, kern, cand, mini, rows2d, cnorm, ncol, mnorm, total, summed,
    own_eig, got_eig, idcol, half_c, half_s, *rest,
):
    bslots = [rest[2 * s : 2 * s + 2] for s in range(3)]
    sslots = [rest[6 + 3 * s : 9 + 3 * s] for s in range(3)]
    send_sems, recv_sems, local_sems = rest[15:]
    chip, core = position()
    other = 1 - core
    links = Links(send_sems, recv_sems)
    sibling = device(chip, other)
    my_nys = lax.axis_index("nys")
    near = chip[0], chip[1], chip[2] + 1 - 2 * lax.rem(chip[2], 2)
    partners = [sibling, device(near, other)]
    for axis in range(3):
        partners += [peer_at(chip, core, axis, step)[1] for step in (1, 2, 3)]

    barrier = pltpu.get_barrier_semaphore()
    for to in partners:
        pl.semaphore_signal(barrier, inc=1, device_id=to, device_id_type=MESH)
    loads = [
        pltpu.make_async_copy(a, b, local_sems.at[i])
        for i, (a, b) in enumerate(((centers_hbm, cent), (weights_hbm, wts), (labels_hbm, labs)))
    ]
    for load in loads:
        load.start()

    away = loader_ref[0] - (lax.axis_index("centers") * 4 + my_nys)
    ids = jnp.minimum(ids_ref[...] + away * away * 4096, 4096).astype(F32)
    idcol[...] = jnp.broadcast_to(ids, (128, BATCH)).T
    own_eig[...] = eig_ref[...].astype(F32)

    def pick_block(block):
        rows = pl.ds(pl.multiple_of(block * 256, 256), 256)
        column_ids = idcol[rows, :].astype(jnp.int32)

        def put(k, _):
            lane = lax.broadcasted_iota(jnp.int32, (256, 128), 1) + k * 128
            pick[rows, pl.ds(pl.multiple_of(k * 128, 128), 128)] = jnp.where(lane == column_ids, 1.0, 0.0).astype(BF16)
            return 0

        lax.fori_loop(0, 16, put, 0, unroll=4)

    def candidate_block(half, s):
        block = half * 2 + s
        pick_block(block)
        rows = pl.ds(pl.multiple_of(block * 256, 256), 256)

        def put(k, _):
            columns = pl.ds(pl.multiple_of(k * 256, 256), 256)
            got = jnp.dot(pick[rows, :], cent[:, columns], preferred_element_type=F32)
            cand[pl.ds(half, 1), pl.ds(s * 2, 2), :, :, columns] = got.astype(BF16).reshape(1, 2, 4, 32, 256)
            return 0

        lax.fori_loop(0, 4, put, 0)
        return 0

    pl.semaphore_wait(barrier, len(partners))
    eig_copies = []
    for to_core, to_chip in ((other, chip), (core, near), (other, near)):
        to = device(to_chip, to_core)
        eig_copies.append(
            links.start(own_eig.at[:, pl.ds(pl.multiple_of(to[1] * 128, 128), 128)], got_eig.at[my_nys], to)
        )
    got_eig[my_nys] = own_eig[:, pl.ds(pl.multiple_of(my_nys * 128, 128), 128)]

    loads[0].wait()
    lax.fori_loop(0, 2, lambda s, _: candidate_block(other, s), 0)
    first = links.start(cand.at[other], half_c, sibling)
    lax.fori_loop(0, 2, lambda s, _: candidate_block(core, s), 0)
    first.wait_recv()

    def add_half(k, _):
        x, y = lax.div(k, 4), lax.rem(k, 4)
        cand[core, x, y] = (cand[core, x, y].astype(F32) + half_c[x, y].astype(F32)).astype(BF16)
        return 0

    lax.fori_loop(0, 16, add_half, 0)
    pick_out = pltpu.make_async_copy(pick, pick_hbm, local_sems.at[3])
    pick_out.start()

    def targets(x):
        def put(k, _):
            columns = pl.ds(pl.multiple_of(k * 256, 256), 256)
            wanted = pick[columns, :]
            if x < 3:
                got = lax.dot_general(labs[pl.ds(x * 320, 320), :], wanted, NT, preferred_element_type=F32)
            else:
                got = lax.dot_general(labs[pl.ds(960, 40), :], wanted, NT, preferred_element_type=F32)
                got = jnp.concatenate([got, jnp.zeros((280, 256), F32)], axis=0)
            total[x, :, :, columns] = got.astype(BF16).reshape(4, 80, 256)
            return 0

        lax.fori_loop(0, 4, put, 0)

    def center_norms():
        def put(k, _):
            rows = pl.ds(pl.multiple_of(k * 64, 64), 64)
            cnorm[rows, :] = jnp.sum(jnp.square(cent[rows, :].astype(F32)), axis=1, keepdims=True)
            return 0

        lax.fori_loop(0, 32, put, 0)

    def stack_rows():
        loads[1].wait()

        def put(k, _):
            rows = pl.ds(pl.multiple_of(k * 64, 64), 64)
            stack[rows, :] = wts[rows, :]
            return 0

        lax.fori_loop(0, 15, put, 0)

    def stack_tail():
        for copy in eig_copies:
            copy.wait_recv()
        vectors = got_eig[...].reshape(Q, NYS_DEV).astype(BF16)
        row_ids = jnp.broadcast_to(nys_ref[...].astype(F32), (128, 128)).T.astype(jnp.int32)

        def put(k, _):
            columns = pl.ds(pl.multiple_of(k * 128, 128), 128)
            lane = lax.broadcasted_iota(jnp.int32, (128, 128), 1) + k * 128
            chosen = jnp.where(lane == row_ids, 1.0, 0.0).astype(BF16)
            spread = jnp.dot(vectors, chosen, preferred_element_type=F32)
            tail = jnp.concatenate(
                [wts[pl.ds(960, 40), columns].astype(F32), jnp.zeros((8, 128), F32), spread, jnp.zeros((112, 128), F32)],
                axis=0,
            )
            stack[pl.ds(960, 320), columns] = tail.astype(BF16)
            return 0

        lax.fori_loop(0, 16, put, 0)

    def nothing():
        pass

    def first_work():
        loads[2].wait()
        targets(0)
        targets(1)
        center_norms()

    def second_work():
        stack_rows()

    def third_work():
        stack_tail()

    flights = [scatter_start(links, cand, bslots[0][p], bcast_index, chip, core, part, 0) for p, part in enumerate(BCAST_PARTS)]
    for stage, work in enumerate((first_work, second_work, third_work)):
        work()
        following = []
        for p, part in enumerate(BCAST_PARTS):
            last = stage == 2
            scatter_finish(
                flights[p], cand, bslots[stage][p], bcast_index, chip, core, part, stage, mini if last else cand
            )
            if last:
                following.append(gather_start(links, mini, bcast_index, chip, core, part, 2))
            else:
                following.append(
                    scatter_start(links, cand, bslots[stage + 1][p], bcast_index, chip, core, part, stage + 1)
                )
        flights = following
    swaps = []
    for stage, work in ((2, lambda: targets(2)), (1, lambda: targets(3)), (0, nothing)):
        work()
        following = []
        for p, part in enumerate(BCAST_PARTS):
            for copy in flights[p]:
                copy.wait_recv()
            if stage > 0:
                following.append(gather_start(links, mini, bcast_index, chip, core, part, stage - 1))
            else:
                whole = mini.at[bcast_index(core, part, {})]
                swaps.append(links.start(whole, whole, sibling))
        flights = following

    def kernel_half(half):
        offset = pl.multiple_of(half * HALF, HALF)

        def rows_of(k, _):
            rows = pl.ds(pl.multiple_of(k * 32, 32), 32)
            block = mini[half, lax.div(k, 4), lax.rem(k, 4)]
            rows2d[rows, :] = block
            norm = jnp.sum(jnp.square(block.astype(F32)), axis=1, keepdims=True)
            ncol[rows, :] = jnp.broadcast_to(norm, (32, 128))
            return 0

        lax.fori_loop(0, 16, rows_of, 0)
        mnorm[...] = ncol[...].T[0:8, :]

        def put(k, _):
            rows = pl.ds(pl.multiple_of(k * 256, 256), 256)
            inner = lax.dot_general(cent[rows, :], rows2d[...], NT, preferred_element_type=F32)
            square = jnp.maximum(cnorm[rows, :] + mnorm[0:1, :] - 2.0 * inner, 0.0)
            kern[rows, pl.ds(offset, HALF)] = jnp.exp(jnp.sqrt(square) * (-1.0 / kernel_width)).astype(BF16)
            return 0

        lax.fori_loop(0, 8, put, 0)

    kernel_half(core)
    for copy in swaps:
        copy.wait_recv()
    kernel_half(other)

    def product(half, x):
        columns = pl.ds(pl.multiple_of(half * HALF, HALF), HALF)
        rows = pl.ds(pl.multiple_of(x * 320, 320), 320)
        got = jnp.dot(stack[rows, :], kern[:, columns], preferred_element_type=F32).reshape(1, 4, 80, HALF)
        return got - total[pl.ds(x, 1), :, :, columns].astype(F32), columns

    halves = []
    for step in (1, 2, 3, 0):
        x = lax.rem(chip[0] + step, 4)
        got, columns = product(other, x)
        total[pl.ds(x, 1), :, :, columns] = got.astype(BF16)
        halves.append(links.start(total.at[pl.ds(x, 1), :, :, columns], half_s.at[pl.ds(x, 1)], sibling))
    flights = [[], [], []]
    for i, step in enumerate((1, 2, 3, 0)):
        x = lax.rem(chip[0] + step, 4)
        got, columns = product(core, x)
        halves[i].wait_recv()
        got += half_s[pl.ds(x, 1)].astype(F32)
        total[pl.ds(x, 1), :, :, columns] = got.astype(BF16)
        if step:
            moved, to = peer_at(chip, core, 0, step)
            flights[0].append(
                links.start(total.at[sum_index(core, SUM_PARTS[0], {0: x})], sslots[0][0].at[step - 1], to)
            )
    for p in (1, 2):
        flights[p] = scatter_start(links, total, sslots[0][p], sum_index, chip, core, SUM_PARTS[p], 0)
    for stage in range(3):
        following = []
        for p, part in enumerate(SUM_PARTS):
            last = stage == 2
            scatter_finish(
                flights[p], total, sslots[stage][p], sum_index, chip, core, part, stage, summed if last else total
            )
            if last:
                following.append(gather_start(links, summed, sum_index, chip, core, part, 2))
            else:
                following.append(
                    scatter_start(links, total, sslots[stage + 1][p], sum_index, chip, core, part, stage + 1)
                )
        flights = following
    swaps = []
    for stage in (2, 1, 0):
        following = []
        for p, part in enumerate(SUM_PARTS):
            for copy in flights[p]:
                copy.wait_recv()
            if stage > 0:
                following.append(gather_start(links, summed, sum_index, chip, core, part, stage - 1))
            else:
                whole = summed.at[sum_index(core, part, {})]
                swaps.append(links.start(whole, whole, sibling))
        flights = following
    spread_out = pltpu.make_async_copy(stack.at[pl.ds(EIG_ROW, Q)], spread_hbm, local_sems.at[4])
    spread_out.start()
    for copy in swaps:
        copy.wait_recv()
    sums_out = pltpu.make_async_copy(summed, sums_hbm, local_sems.at[5])
    sums_out.start()
    links.wait_sends()
    pick_out.wait()
    spread_out.wait()
    sums_out.wait()


def update_kernel(weights_ref, part_ref, eig_ref, scale_ref, pick_ref, spread_ref, out_ref, residual_ref):
    part = part_ref[...]
    reduced = lax.dot_general(part, eig_ref[...], NT, preferred_element_type=F32)
    coefficients = (reduced * scale_ref[...]).astype(BF16)
    step = jnp.dot(coefficients, spread_ref[...], preferred_element_type=F32)
    step -= jnp.dot(part, pick_ref[...], preferred_element_type=F32)
    out_ref[...] = (weights_ref[...].astype(F32) + learn_rate * step).astype(BF16)
    residual_ref[...] = part


def body(centers, weights, labels, loader, sample_ids, nys_ids, eigen_vectors, eigen_scale):
    vmem, anywhere = pl.BlockSpec(memory_space=pltpu.VMEM), pl.BlockSpec(memory_space=pl.ANY)
    weights_t = weights.T
    scratch = [
        pltpu.VMEM((C_DEV, D), BF16),
        pltpu.VMEM((OUT, C_DEV), BF16),
        pltpu.VMEM((OUT, C_DEV), BF16),
        pltpu.VMEM((BATCH, C_DEV), BF16),
        pltpu.VMEM((ROWS, C_DEV), BF16),
        pltpu.VMEM((C_DEV, BATCH), BF16),
        pltpu.VMEM((2, 4, 4, 32, D), BF16),
        pltpu.VMEM((2, 4, 4, 32, D), BF16),
        pltpu.VMEM((HALF, D), BF16),
        pltpu.VMEM((C_DEV, 1), F32),
        pltpu.VMEM((HALF, 128), F32),
        pltpu.VMEM((8, HALF), F32),
        pltpu.VMEM((4, 4, 80, BATCH), BF16),
        pltpu.VMEM((4, 4, 80, BATCH), BF16),
        pltpu.VMEM((40, 512), F32),
        pltpu.VMEM((4, 40, 128), F32),
        pltpu.VMEM((BATCH, 128), F32),
        pltpu.VMEM((4, 4, 32, D), BF16),
        pltpu.VMEM((4, 4, 80, HALF), BF16),
    ]
    for stage in range(3):
        scratch += [pltpu.VMEM((3,) + bcast_shape(part, part[1][: stage + 1]), BF16) for part in BCAST_PARTS]
    for stage in range(3):
        scratch += [pltpu.VMEM((3,) + sum_shape(part, part[1][: stage + 1]), BF16) for part in SUM_PARTS]
    count = 3 + 1 + 36 + 2 + 4 + 54 + 3
    scratch += [pltpu.SemaphoreType.DMA((count,)), pltpu.SemaphoreType.DMA((count,)), pltpu.SemaphoreType.DMA((6,))]
    sums, pick, spread = pl.pallas_call(
        step_kernel,
        out_shape=(
            jax.ShapeDtypeStruct((4, 4, 80, BATCH), BF16),
            jax.ShapeDtypeStruct((BATCH, C_DEV), BF16),
            jax.ShapeDtypeStruct((Q, C_DEV), BF16),
        ),
        in_specs=[pl.BlockSpec(memory_space=pltpu.SMEM), vmem, vmem, vmem, anywhere, anywhere, anywhere],
        out_specs=(anywhere, anywhere, anywhere),
        scratch_shapes=scratch,
        compiler_params=pltpu.CompilerParams(
            collective_id=0, has_side_effects=True, vmem_limit_bytes=58 * 2**20
        ),
        name="step",
    )(loader, sample_ids.reshape(1, BATCH), nys_ids.reshape(1, NYS_DEV), eigen_vectors.T, centers, weights_t, labels.T)
    sums = sums.reshape(ROWS, BATCH)
    new_weights, residual = pl.pallas_call(
        update_kernel,
        grid=(4,),
        out_shape=(jax.ShapeDtypeStruct((OUT, C_DEV), BF16), jax.ShapeDtypeStruct((OUT, BATCH), BF16)),
        in_specs=[
            pl.BlockSpec((256, C_DEV), lambda i: (i, 0)),
            pl.BlockSpec((256, BATCH), lambda i: (i, 0)),
            pl.BlockSpec((Q, BATCH), lambda i: (0, 0)),
            pl.BlockSpec((1, Q), lambda i: (0, 0)),
            pl.BlockSpec((BATCH, C_DEV), lambda i: (0, 0)),
            pl.BlockSpec((Q, C_DEV), lambda i: (0, 0)),
        ],
        out_specs=(
            pl.BlockSpec((256, C_DEV), lambda i: (i, 0)),
            pl.BlockSpec((256, BATCH), lambda i: (i, 0)),
        ),
        compiler_params=pltpu.CompilerParams(vmem_limit_bytes=40 * 2**20),
        name="update",
    )(weights_t, sums, lax.slice_in_dim(sums, EIG_ROW, EIG_ROW + Q, axis=0), eigen_scale.reshape(1, Q), pick, spread)
    return (new_weights.T, residual.T)


def solution(mesh):
    placed = (
        P(("centers", "nys"), None),
        P(("centers", "nys"), None),
        P(("centers", "nys"), None),
        P(),
        P(),
        P(("centers", "nys")),
        P("centers", "nys"),
        P(),
    )
    return jax.shard_map(
        body,
        mesh=mesh,
        in_specs=placed,
        out_specs=(P(("centers", "nys"), None), P()),
        check_vma=False,
    )
```

time: 489 us -> 119 us (0.24)
  waiting for transfers between devices: 251 us -> 0 us
  Pallas kernels: 0 us -> 112 us
  blocking collectives: 110 us -> 0 us
  other arithmetic: 42.1 us -> 0 us
  local copies, waits for them, and re-layouts: 46.9 us -> 6.01 us
  matrix products: 21.9 us -> 0 us
  between operations: 14.8 us -> 1.33 us
    psum x2 -> x0, waiting for transfers between devices: 251 us -> none  [the longest x1 136 us: body(): reduced = lax.psum(local_coef, ('centers', 'nys'))]
    pallas_call x0 -> x2, Pallas kernels: none -> 112 us  [the longest x1 102 us: body(): pl.pallas_call(step_kernel, out_shape=(jax.ShapeDtypeStruct((4, 4, 80, BA...]
    psum x1 -> x0, blocking collectives: 103 us -> none  [body(): summed_rows = lax.psum(predicted - target_term, ('centers', 'nys'))]
    scatter-add x2 -> x0, other arithmetic: 25 us -> none  [the longest x1 16.9 us: body(): weight_step.at[sample_ids].add(batch_scale * residual.astype(jnp.float32))]
    dot_general x4 -> x0, matrix products: 21.9 us -> none  [the longest x1 15.2 us: body(): jnp.dot(kernel_rows, weights, preferred_element_type=jnp.float32)]
    gather x4 -> x0, local copies, waits for them, and re-layouts: 21.6 us -> none  [the longest x2 10.1 us: body(): targets = jnp.take(labels, sample_ids, axis=0).astype(jnp.float32)]
    unnamed x12 -> x10, local copies, waits for them, and re-layouts: 12.9 us -> 5.02 us
    all_gather x1 -> x0, blocking collectives: 7.57 us -> none  [body(): eigen_block = lax.all_gather(eigen_vectors, 'nys', axis=1, tiled=True)]
  transfers between devices with their start and end apart: 2 -> 0, of which waited for: 2 -> 0; matrix products, arithmetic and copies ran while one was open for 8% -> 0% of each run, Pallas kernels for 0% -> 0%
where the time goes in v1:
time: 119 us
  Pallas kernels  112 us (94%)
  local copies, waits for them, and re-layouts  6.01 us (5%)
  between operations  1.33 us (1%)
    pallas_call x1, Pallas kernels, body(): pl.pallas_call(step_kernel, out_shape=(jax.ShapeDtypeStruct((4, 4, 80, BA...  102 us
    pallas_call x1, Pallas kernels, body(): pl.pallas_call(update_kernel, grid=(4,), out_shape=(jax.ShapeDtypeStruct(...  9.44 us
    unnamed x10, local copies, waits for them, and re-layouts  5.02 us

profile of v1, /device:TPU:1, one launch (start us, length us, event | category | flops | bytes accessed | tf_op | source)
XLA Modules:
  0.0 118.9 jit_solution(13498441295201385448)
XLA Ops:
  1.3 0.0 copy-start
  1.3 0.0 copy-start.4
  1.3 102.2 %step.1 = (bf16[4,4,80,1024]{3,2,1,0:T(8,128)(2,1)}, bf16[1024,2048]{1,0:T(8,128)(2,1)}, bf16[160,2048]{1,0:T(8,128)(2,1)}) custom-call(s32[1]{0:T(128)S(6)} %copy.10.loader_ref, s32[1,1024]{1,0:T(1,128)} %bitcast.16, s32[1,128]{1,0:T(1,128)} %bitcast.17, bf16[40,512]{1,0:T(8,128)(2,1)} %bitcast.15, bf16[2048,1024]{1,0:T(8,128)(2,1)} %centers_hbm.1, ...), custom_call_target="tpu_custom_call" | custom-call | tf_op jit(solution)/shard_map/step/pallas_call | solution.py:430
  103.5 1.0 slice.4.eig_ref
  104.5 0.0 copy-done
  104.5 0.0 copy-done.4
  104.5 0.0 copy-start.1
  104.5 2.2 %copy-done.1 = bf16[1024,2048]{1,0:T(8,128)(2,1)S(1)} copy-done((bf16[1024,2048]{1,0:T(8,128)(2,1)S(1)}, bf16[1024,2048]{1,0:T(8,128)(2,1)}, u32[]{:S(2)}) %copy-start.1) | copy-done | bytes 4194328
  106.7 0.0 copy-start.2
  106.7 1.7 %copy-done.2 = bf16[4,4,80,1024]{3,2,1,0:T(8,128)(2,1)S(1)} copy-done((bf16[4,4,80,1024]{3,2,1,0:T(8,128)(2,1)S(1)}, bf16[4,4,80,1024]{3,2,1,0:T(8,128)(2,1)}, u32[]{:S(2)}) %copy-start.2) | copy-done | bytes 2621464
  108.4 0.0 copy-start.3
  108.4 1.1 copy-done.3
  109.5 9.4 %update.1 = (bf16[1000,2048]{1,0:T(8,128)(2,1)}, bf16[1000,1024]{1,0:T(8,128)(2,1)}) custom-call(bf16[1000,2048]{1,0:T(8,128)(2,1)S(1)} %bitcast.10, bf16[1280,1024]{1,0:T(8,128)(2,1)S(1)} %bitcast.12, bf16[160,1024]{1,0:T(8,128)(2,1)S(1)} %slice.4.eig_ref, f32[1,160]{1,0:T(1,128)S(1)} %bitcast.13, bf16[1024,2048]{1,0:T(8,128)(2,1)S(1)} %copy-done.1, ...), custom_call_target="tpu_custom_call" | custom-call | tf_op jit(solution)/shard_map/update/pallas_call | solution.py:446
Async XLA Ops:
  1.3 103.2 %copy-start = (bf16[2048,1000]{0,1:T(8,128)(2,1)S(1)}, bf16[2048,1000]{0,1:T(8,128)(2,1)}, u32[]{:S(2)}) copy-start(bf16[2048,1000]{0,1:T(8,128)(2,1)} %param.9) | copy-start | bytes 12288004
  1.3 103.2 %copy-start.4 = (f32[160]{0:T(256)S(1)}, f32[160]{0:T(256)}, u32[]{:S(2)}) copy-start(f32[160]{0:T(256)} %param.15) | copy-start | bytes 1924
  104.5 2.2 %copy-start.1 = (bf16[1024,2048]{1,0:T(8,128)(2,1)S(1)}, bf16[1024,2048]{1,0:T(8,128)(2,1)}, u32[]{:S(2)}) copy-start(bf16[1024,2048]{1,0:T(8,128)(2,1)} %get-tuple-element.8.pick_ref) | copy-start | bytes 12582916
  106.7 1.7 %copy-start.2 = (bf16[4,4,80,1024]{3,2,1,0:T(8,128)(2,1)S(1)}, bf16[4,4,80,1024]{3,2,1,0:T(8,128)(2,1)}, u32[]{:S(2)}) copy-start(bf16[4,4,80,1024]{3,2,1,0:T(8,128)(2,1)} %get-tuple-element.7) | copy-start | bytes 7864324
  108.4 1.1 copy-start.3

commit v2 on v0

v2 whole, which is shorter than its diff:
```python
import jax
import jax.numpy as jnp
from jax import lax
from jax.experimental import pallas as pl
from jax.experimental.pallas import tpu as pltpu
from jax.sharding import PartitionSpec as P

MESH = pl.DeviceIdType.MESH
BF16, F32 = jnp.bfloat16, jnp.float32

learn_rate = 0.5
kernel_width = 0.25

D, OUT, Q, BATCH, C_DEV, NYS_DEV = 1024, 1000, 160, 1024, 2048, 128
QUARTER = BATCH // 4
ROWS = 1280
EIG_ROW = 1008
BCAST_PARTS = (((0, 384), (0, 1, 2)), ((384, 384), (1, 2, 0)), ((768, 256), (2, 0, 1)))
SUM_PARTS = (((0, 32), (0, 1, 2)), ((512, 32), (1, 2, 0)), ((1024, 16), (2, 0, 1)))
NT = (((1,), (1,)), ((), ()))


def position():
    c, n = lax.axis_index("centers"), lax.axis_index("nys")
    x, y = lax.rem(c, 4), lax.div(c, 8)
    z = lax.rem(lax.div(c, 4), 2) * 2 + lax.div(n, 2)
    return (x, y, z), lax.rem(n, 2)


def device(chip, core):
    x, y, z = chip
    return ((y * 2 + lax.div(z, 2)) * 4 + x, lax.rem(z, 2) * 2 + core)


def peer_at(chip, core, axis, step):
    moved = list(chip)
    moved[axis] = lax.rem(chip[axis] + step, 4)
    return moved[axis], device(moved, core)


def span(value, count):
    return pl.ds(pl.multiple_of(value * count, count), count)


def bcast_index(quarter, part, v0, v1=None):
    (first, count), _ = part
    second = pl.ds(0, 4) if v1 is None else pl.ds(v1, 1)
    return (pl.ds(quarter, 1), second, pl.ds(v0, 1), pl.ds(0, 16), pl.ds(first, count))


def sum_index(quarter, part, v0, v1=None):
    (first, count), _ = part
    start, rows = (v0 * 4 * count, 4 * count) if v1 is None else ((v0 * 4 + v1) * count, count)
    return (pl.ds(quarter, 1), pl.ds(pl.multiple_of(first + start, 16), rows), pl.ds(0, QUARTER))


def bcast_shape(part, stage):
    return (1, 4 if stage == 0 else 1, 1, 16, part[0][1])


def sum_shape(part, stage):
    return (1, part[0][1] * (4 if stage == 0 else 1), QUARTER)


class Links:
    def __init__(self, core, send_sems, recv_sems):
        self.core, self.send_sems, self.recv_sems, self.copies = core, send_sems, recv_sems, []

    def start(self, source, target, to):
        i = len(self.copies)
        copy = pltpu.make_async_remote_copy(
            src_ref=source, dst_ref=target, send_sem=self.send_sems.at[i], recv_sem=self.recv_sems.at[i],
            device_id=to, device_id_type=MESH,
        )
        copy.start()
        self.copies.append(copy)
        return copy

    def wait_sends(self):
        for copy in self.copies:
            copy.wait_send()


STEPS = (2, 1, 3)


class Reduction:
    def __init__(self, links, index, parts, buffer, result, slots, chip, quarter):
        self.links, self.index, self.parts, self.buffer, self.result = links, index, parts, buffer, result
        self.slots, self.chip, self.quarter = slots, chip, quarter
        self.flights = [[] for _ in parts]

    def at(self, p, *places):
        return self.index(self.quarter, self.parts[p], *places)

    def own(self, p, count):
        return self.at(p, *(self.chip[a] for a in self.parts[p][1][:count]))

    def peer(self, p, stage, step):
        return peer_at(self.chip, self.links.core, self.parts[p][1][stage], step)

    def scatter_first(self, p, step):
        place, to = self.peer(p, 0, step)
        self.flights[p].append(self.links.start(self.buffer.at[self.at(p, place)], self.slots[0][p].at[step - 1], to))

    def scatter_all(self):
        for p in range(len(self.parts)):
            for step in STEPS:
                self.scatter_first(p, step)

    def arrive(self, p):
        for copy in self.flights[p]:
            copy.wait_recv()

    def add(self, p, stage):
        self.arrive(p)
        own = self.own(p, stage + 1)
        got = self.buffer[own].astype(F32)
        for step in range(3):
            got += self.slots[stage][p][step].astype(F32)
        return own, got.astype(BF16)

    def send(self, p, stage, ref):
        self.flights[p] = [self.links.start(ref, ref, self.peer(p, stage, step)[1]) for step in STEPS]

    def second(self):
        for p in range(len(self.parts)):
            own, got = self.add(p, 0)
            self.buffer[own] = got
            mine, self.flights[p] = self.chip[self.parts[p][1][0]], []
            for step in STEPS:
                place, to = self.peer(p, 1, step)
                self.flights[p].append(
                    self.links.start(self.buffer.at[self.at(p, mine, place)], self.slots[1][p].at[step - 1], to)
                )

    def exchange(self):
        for p in range(len(self.parts)):
            _, got = self.add(p, 1)
            place = self.chip[self.parts[p][1][2]]
            self.slots[2][p][place] = got
            self.send(p, 2, self.slots[2][p].at[place])

    def gather_second(self):
        for p in range(len(self.parts)):
            self.arrive(p)
            got = self.slots[2][p][0].astype(F32)
            for place in range(1, 4):
                got += self.slots[2][p][place].astype(F32)
            own = self.own(p, 2)
            self.result[own] = got.astype(BF16)
            self.send(p, 1, self.result.at[own])

    def gather_first(self):
        for p in range(len(self.parts)):
            self.arrive(p)
            self.send(p, 0, self.result.at[self.own(p, 1)])

    def swap(self, sibling):
        for p in range(len(self.parts)):
            self.arrive(p)
        ref = self.result.at[self.quarter]
        return self.links.start(ref, ref, sibling)


def step_kernel(
    loader_ref, ids_ref, nys_ref, eig_ref, scale_ref, centers_hbm, weights_hbm, labels_hbm,
    new_hbm, res_hbm,
    cent, wts, labs, pick, stack, kern, cand, mini, cnorm, ncol, mnorm, total, summed,
    own_eig, got_eig, idcol, half_c, half_s, steps, partial, *rest,
):
    bslots = [[rest[9 * u + 3 * s : 9 * u + 3 * s + 3] for s in range(3)] for u in range(2)]
    sslots = [[rest[18 + 9 * u + 3 * s : 21 + 9 * u + 3 * s] for s in range(3)] for u in range(2)]
    send_sems, recv_sems, local_sems = rest[36:]
    chip, core = position()
    other = 1 - core
    links = Links(core, send_sems, recv_sems)
    sibling = device(chip, other)
    my_nys = lax.axis_index("nys")
    near = chip[0], chip[1], chip[2] + 1 - 2 * lax.rem(chip[2], 2)
    partners = [sibling, device(near, other)]
    for axis in range(3):
        partners += [peer_at(chip, core, axis, step)[1] for step in (1, 2, 3)]

    barrier = pltpu.get_barrier_semaphore()
    for to in partners:
        pl.semaphore_signal(barrier, inc=1, device_id=to, device_id_type=MESH)
    loads = [
        pltpu.make_async_copy(a, b, local_sems.at[i])
        for i, (a, b) in enumerate(((centers_hbm, cent), (weights_hbm, wts), (labels_hbm, labs)))
    ]
    loads[0].start()

    away = loader_ref[0] - (lax.axis_index("centers") * 4 + my_nys)
    ids = jnp.minimum(ids_ref[...] + away * away * 4096, 4096).astype(F32)
    idcol[...] = jnp.broadcast_to(ids, (128, BATCH)).T
    own_eig[...] = eig_ref[...].astype(F32)

    def pick_block(block):
        rows = span(block, 256)
        column_ids = idcol[rows, :].astype(jnp.int32)

        def put(k, _):
            lane = lax.broadcasted_iota(jnp.int32, (256, 128), 1) + k * 128
            pick[rows, span(k, 128)] = jnp.where(lane == column_ids, 1.0, 0.0).astype(BF16)
            return 0

        lax.fori_loop(0, 16, put, 0, unroll=4)

    def candidates(quarter):
        rows = span(quarter, 256)

        def put(k, _):
            columns = span(k, 256)
            got = jnp.dot(pick[rows, :], cent[:, columns], preferred_element_type=F32)
            cand[pl.ds(quarter, 1), :, :, :, columns] = got.astype(BF16).reshape(1, 4, 4, 16, 256)
            return 0

        lax.fori_loop(0, 4, put, 0)

    batch = [Reduction(links, bcast_index, BCAST_PARTS, cand, mini, bslots[u], chip, u * 2 + core) for u in range(2)]
    sums = [Reduction(links, sum_index, SUM_PARTS, total, summed, sslots[u], chip, u * 2 + core) for u in range(2)]
    eig_copies = []
    pick_block(other)
    for u in range(2):
        mine, theirs = u * 2 + core, u * 2 + other
        if u == 0:
            loads[0].wait()
            loads[1].start()
            loads[2].start()
        candidates(theirs)
        if u == 0:
            pl.semaphore_wait(barrier, len(partners))
        first = links.start(cand.at[theirs], half_c.at[u], sibling)
        if u == 0:
            for to_core, to_chip in ((other, chip), (core, near), (other, near)):
                to = device(to_chip, to_core)
                eig_copies.append(links.start(own_eig.at[:, span(to[1], 128)], got_eig.at[my_nys], to))
            got_eig[my_nys] = own_eig[:, span(my_nys, 128)]
        pick_block(mine)
        candidates(mine)
        if u == 0:
            pick_block(2 + other)
        first.wait_recv()

        def add_half(k, _):
            cand[mine, k] = (cand[mine, k].astype(F32) + half_c[u, k].astype(F32)).astype(BF16)
            return 0

        lax.fori_loop(0, 4, add_half, 0)
        batch[u].scatter_all()
    def targets(x):
        def put(k, _):
            wanted = pick[span(k, 256), :]
            if x < 3:
                got = lax.dot_general(labs[pl.ds(x * 320, 320), :], wanted, NT, preferred_element_type=F32)
            else:
                got = lax.dot_general(labs[pl.ds(960, 40), :], wanted, NT, preferred_element_type=F32)
                got = jnp.concatenate([got, jnp.zeros((280, 256), F32)], axis=0)
            total[k, pl.ds(x * 320, 320), :] = got.astype(BF16)
            return 0

        lax.fori_loop(0, 4, put, 0)

    def center_norms():
        def put(k, _):
            rows = span(k, 64)
            norm = jnp.sum(jnp.square(cent[rows, :].astype(F32)), axis=1, keepdims=True)
            cnorm[rows, :] = jnp.broadcast_to(norm, (64, 128))
            return 0

        lax.fori_loop(0, 32, put, 0)

    def stack_rows():
        loads[1].wait()

        def put(k, _):
            rows = span(k, 64)
            stack[rows, :] = wts[rows, :]
            return 0

        lax.fori_loop(0, 15, put, 0)

    def stack_tail():
        for copy in eig_copies:
            copy.wait_recv()
        vectors = got_eig[...].reshape(Q, NYS_DEV).astype(BF16)
        row_ids = jnp.broadcast_to(nys_ref[...].astype(F32), (128, 128)).T.astype(jnp.int32)

        def put(k, _):
            columns = span(k, 128)
            lane = lax.broadcasted_iota(jnp.int32, (128, 128), 1) + k * 128
            chosen = jnp.where(lane == row_ids, 1.0, 0.0).astype(BF16)
            spread = jnp.dot(vectors, chosen, preferred_element_type=F32)
            tail = jnp.concatenate(
                [wts[pl.ds(960, 40), columns].astype(F32), jnp.zeros((8, 128), F32), spread, jnp.zeros((112, 128), F32)],
                axis=0,
            )
            stack[pl.ds(960, 320), columns] = tail.astype(BF16)
            return 0

        lax.fori_loop(0, 16, put, 0)

    def kernel_quarter(quarter, midway=None):
        def rows_of(k, _):
            block = mini[quarter, k].reshape(64, D)
            norm = jnp.sum(jnp.square(block.astype(F32)), axis=1, keepdims=True)
            ncol[span(k, 64), :] = jnp.broadcast_to(norm, (64, 128))
            return 0

        lax.fori_loop(0, 4, rows_of, 0)
        mnorm[...] = ncol[...].T[0:8, :]

        def inner(k):
            rows = mini[quarter].reshape(256, D)
            return lax.dot_general(cent[pl.ds(k * 256, 256), :], rows, NT, preferred_element_type=F32)

        following = inner(0)
        for k in range(8):
            current = following
            if k < 7:
                following = inner(k + 1)
            if k == 4 and midway is not None:
                midway()
            rows = pl.ds(k * 256, 256)
            for j in range(2):
                lanes = pl.ds(j * 128, 128)
                square = cnorm[rows, :] + mnorm[0:1, lanes] - 2.0 * current[:, j * 128 : (j + 1) * 128]
                square = jnp.minimum(jnp.maximum(square, 1e-30), 3e38)
                distance = square * lax.rsqrt(square)
                kern[quarter, rows, lanes] = jnp.exp(distance * (-1.0 / kernel_width)).astype(BF16)

    def product(quarter, step):
        places = [lax.rem(chip[axes[0]] + step, 4) for _, axes in SUM_PARTS]
        slices = [sum_index(quarter, part, place)[1] for part, place in zip(SUM_PARTS, places)]
        rows = jnp.concatenate([stack[at, :] for at in slices], axis=0)
        got = jnp.dot(rows, kern[quarter], preferred_element_type=F32)
        pieces, start = [], 0
        for part, at in zip(SUM_PARTS, slices):
            count = 4 * part[0][1]
            pieces.append((at, got[start : start + count] - total[quarter, at, :].astype(F32)))
            start += count
        return pieces

    def their_products(u):
        copies = []
        for step in STEPS + (0,):
            copies.append([])
            for at, got in product(u * 2 + other, step):
                ref = total.at[u * 2 + other, at, :]
                ref[...] = got.astype(BF16)
                copies[-1].append(links.start(ref, half_s.at[u, at, :], sibling))
        return copies

    def own_products(u, copies):
        for i, step in enumerate(STEPS + (0,)):
            for p, (at, got) in enumerate(product(u * 2 + core, step)):
                copies[i][p].wait_recv()
                total[u * 2 + core, at, :] = (got + half_s[u, at, :].astype(F32)).astype(BF16)
                if step:
                    sums[u].scatter_first(p, step)

    def residual_of(u):
        return jnp.concatenate([summed[2 * u, pl.ds(0, EIG_ROW), :], summed[2 * u + 1, pl.ds(0, EIG_ROW), :]], axis=1)

    def reduced_of(u):
        eigs = [summed[2 * u + h, pl.ds(EIG_ROW, Q), :] for h in range(2)]
        return lax.dot_general(residual_of(u), jnp.concatenate(eigs, axis=1), NT, preferred_element_type=F32)

    def taken(u, k):
        return jnp.dot(residual_of(u), pick[pl.ds(u * 512, 512), pl.ds(k * 512, 512)], preferred_element_type=F32)

    def residual_out(u):
        outs = []
        for q in (2 * u, 2 * u + 1):
            columns = pl.ds(q * 256, 256)
            labs[:, columns] = summed[q, pl.ds(0, OUT), :]
            outs.append(pltpu.make_async_copy(labs.at[:, columns], res_hbm.at[:, columns], local_sems.at[3 + q]))
            outs[-1].start()
        return outs

    stack_rows()
    stack_tail()
    loads[2].wait()
    targets(0)
    for chunk in batch:
        chunk.second()
    targets(1)
    for chunk in batch:
        chunk.exchange()
    targets(2)
    for chunk in batch:
        chunk.gather_second()
    targets(3)
    for chunk in batch:
        chunk.gather_first()
    center_norms()
    swaps = [batch[0].swap(sibling)]
    kernel_quarter(core)
    swaps[0].wait_recv()
    swaps.append(batch[1].swap(sibling))
    kernel_quarter(other)
    own_products(0, their_products(0))
    kernel_quarter(2 + core)
    swaps[1].wait_recv()
    kernel_quarter(2 + other, sums[0].second)
    copies = their_products(1)
    sums[0].exchange()
    own_products(1, copies)
    sums[0].gather_second()
    sums[1].second()
    sums[0].gather_first()
    sums[1].exchange()
    sums[1].gather_second()
    first = sums[0].swap(sibling)
    first.wait_recv()
    outs = residual_out(0)
    for k in range(2):
        steps[:, pl.ds(k * 512, 512)] = taken(0, k)
    sums[1].gather_first()
    for k in range(2, 4):
        steps[:, pl.ds(k * 512, 512)] = taken(0, k)
    partial[...] = reduced_of(0)
    first = sums[1].swap(sibling)
    first.wait_recv()
    outs += residual_out(1)
    coefficients = ((partial[...] + reduced_of(1)) * scale_ref[...]).astype(BF16)
    for k in range(4):
        columns = pl.ds(k * 512, 512)
        step = jnp.dot(coefficients, stack[pl.ds(EIG_ROW, Q), columns], preferred_element_type=F32)
        step -= steps[:, columns] + taken(1, k)
        wts[:, columns] = (wts[:, columns].astype(F32) + learn_rate * step[:OUT]).astype(BF16)
        out = pltpu.make_async_copy(wts.at[:, columns], new_hbm.at[:, columns], local_sems.at[7 + k])
        out.start()
        outs.append(out)
    links.wait_sends()
    for out in outs:
        out.wait()


def body(centers, weights, labels, loader, sample_ids, nys_ids, eigen_vectors, eigen_scale):
    vmem, anywhere = pl.BlockSpec(memory_space=pltpu.VMEM), pl.BlockSpec(memory_space=pl.ANY)
    scratch = [
        pltpu.VMEM((C_DEV, D), BF16),
        pltpu.VMEM((OUT, C_DEV), BF16),
        pltpu.VMEM((OUT, C_DEV), BF16),
        pltpu.VMEM((BATCH, C_DEV), BF16),
        pltpu.VMEM((ROWS, C_DEV), BF16),
        pltpu.VMEM((4, C_DEV, QUARTER), BF16),
        pltpu.VMEM((4, 4, 4, 16, D), BF16),
        pltpu.VMEM((4, 4, 4, 16, D), BF16),
        pltpu.VMEM((C_DEV, 128), F32),
        pltpu.VMEM((256, 128), F32),
        pltpu.VMEM((8, 256), F32),
        pltpu.VMEM((4, ROWS, QUARTER), BF16),
        pltpu.VMEM((4, ROWS, QUARTER), BF16),
        pltpu.VMEM((40, 512), F32),
        pltpu.VMEM((4, 40, 128), F32),
        pltpu.VMEM((BATCH, 128), F32),
        pltpu.VMEM((2, 4, 4, 16, D), BF16),
        pltpu.VMEM((2, ROWS, QUARTER), BF16),
        pltpu.VMEM((EIG_ROW, C_DEV), F32),
        pltpu.VMEM((EIG_ROW, Q), F32),
    ]
    for parts, shape in ((BCAST_PARTS, bcast_shape), (SUM_PARTS, sum_shape)):
        for stage in (0, 1, 2, 0, 1, 2):
            scratch += [pltpu.VMEM((3 + stage // 2,) + shape(part, stage), BF16) for part in parts]
    count = 3 + 2 * (1 + 45 + 1) + 2 * (12 + 45 + 1)
    scratch += [pltpu.SemaphoreType.DMA((count,)), pltpu.SemaphoreType.DMA((count,)), pltpu.SemaphoreType.DMA((11,))]
    new_weights, residual = pl.pallas_call(
        step_kernel,
        out_shape=(
            jax.ShapeDtypeStruct((OUT, C_DEV), BF16),
            jax.ShapeDtypeStruct((OUT, BATCH), BF16),
        ),
        in_specs=[pl.BlockSpec(memory_space=pltpu.SMEM), vmem, vmem, vmem, vmem, anywhere, anywhere, anywhere],
        out_specs=(anywhere, anywhere),
        scratch_shapes=scratch,
        compiler_params=pltpu.CompilerParams(
            collective_id=0, has_side_effects=True, vmem_limit_bytes=62 * 2**20
        ),
        name="step",
    )(
        loader, sample_ids.reshape(1, BATCH), nys_ids.reshape(1, NYS_DEV), eigen_vectors.T, eigen_scale.reshape(1, Q),
        centers, weights.T, labels.T,
    )
    return (new_weights.T, residual.T)


def solution(mesh):
    placed = (
        P(("centers", "nys"), None),
        P(("centers", "nys"), None),
        P(("centers", "nys"), None),
        P(),
        P(),
        P(("centers", "nys")),
        P("centers", "nys"),
        P(),
    )
    return jax.shard_map(
        body,
        mesh=mesh,
        in_specs=placed,
        out_specs=(P(("centers", "nys"), None), P()),
        check_vma=False,
    )
```

time: 489 us -> 98.2 us (0.20)
  waiting for transfers between devices: 251 us -> 0 us
  blocking collectives: 110 us -> 0 us
  Pallas kernels: 0 us -> 90.6 us
  other arithmetic: 42.1 us -> 0 us
  local copies, waits for them, and re-layouts: 46.9 us -> 6.15 us
  matrix products: 21.9 us -> 0 us
  between operations: 14.8 us -> 1.29 us
    psum x2 -> x0, waiting for transfers between devices: 251 us -> none  [the longest x1 136 us: body(): reduced = lax.psum(local_coef, ('centers', 'nys'))]
    psum x1 -> x0, blocking collectives: 103 us -> none  [body(): summed_rows = lax.psum(predicted - target_term, ('centers', 'nys'))]
    pallas_call x0 -> x1, Pallas kernels: none -> 90.6 us  [body(): pl.pallas_call(step_kernel, out_shape=(jax.ShapeDtypeStruct((OUT, C_DEV),...]
    scatter-add x2 -> x0, other arithmetic: 25 us -> none  [the longest x1 16.9 us: body(): weight_step.at[sample_ids].add(batch_scale * residual.astype(jnp.float32))]
    dot_general x4 -> x0, matrix products: 21.9 us -> none  [the longest x1 15.2 us: body(): jnp.dot(kernel_rows, weights, preferred_element_type=jnp.float32)]
    gather x4 -> x0, local copies, waits for them, and re-layouts: 21.6 us -> none  [the longest x2 10.1 us: body(): targets = jnp.take(labels, sample_ids, axis=0).astype(jnp.float32)]
    all_gather x1 -> x0, blocking collectives: 7.57 us -> none  [body(): eigen_block = lax.all_gather(eigen_vectors, 'nys', axis=1, tiled=True)]
    convert_element_type x1 -> x0, local copies, waits for them, and re-layouts: 6.88 us -> none  [body(): weights.astype(jnp.float32) + weight_step]
  transfers between devices with their start and end apart: 2 -> 0, of which waited for: 2 -> 0; matrix products, arithmetic and copies ran while one was open for 8% -> 0% of each run, Pallas kernels for 0% -> 0%
where the time goes in v2:
time: 98.2 us; the launch traced here: 98 us
  Pallas kernels  90.6 us (92%)
  local copies, waits for them, and re-layouts  6.15 us (6%)
  between operations  1.29 us (1%)
    pallas_call x1, Pallas kernels, body(): pl.pallas_call(step_kernel, out_shape=(jax.ShapeDtypeStruct((OUT, C_DEV),...  90.6 us
    unnamed x4, local copies, waits for them, and re-layouts  6.15 us

profile of v2, /device:TPU:1, one launch (start us, length us, event | category | flops | bytes accessed | tf_op | source)
XLA Modules:
  0.0 98.0 jit_solution(7174875014233406506)
XLA Ops:
  1.3 90.6 %step.1 = (bf16[1000,2048]{1,0:T(8,128)(2,1)}, bf16[1000,1024]{1,0:T(8,128)(2,1)}) custom-call(s32[1]{0:T(128)S(6)} %copy.12.loader_ref, s32[1,1024]{1,0:T(1,128)} %bitcast.13, s32[1,128]{1,0:T(1,128)} %bitcast.15, bf16[40,512]{1,0:T(8,128)(2,1)} %bitcast.12, f32[1,160]{1,0:T(1,128)} %bitcast.14, bf16[2048,1024]{1,0:T(8,128)(2,1)} %centers_hbm.1, ...), custom_call_target="tpu_custom_call" | custom-call | tf_op jit(solution)/shard_map/step/pallas_call | solution.py:470
  91.8 0.0 copy-start
  91.9 4.8 %copy.13 = bf16[2048,1000]{0,1:T(8,128)(2,1)} copy(bf16[2048,1000]{0,1:T(8,128)(2,1)} %bitcast.8) | data formatting | bytes 8192000
  96.7 0.0 copy-done
  96.7 1.3 %copy.14 = bf16[1024,1000]{0,1:T(8,128)(2,1)} copy(bf16[1024,1000]{0,1:T(8,128)(2,1)S(1)} %bitcast.11) | data formatting | bytes 4096000
Async XLA Ops:
  91.8 4.9 %copy-start = (bf16[1000,1024]{1,0:T(8,128)(2,1)S(1)}, bf16[1000,1024]{1,0:T(8,128)(2,1)}, u32[]{:S(2)}) copy-start(bf16[1000,1024]{1,0:T(8,128)(2,1)} %get-tuple-element.5) | copy-start | bytes 6144004

commit v3 on v2

--- a/solution.py
+++ b/solution.py
@@ -64,10 +64,10 @@
 
 class Links:
     def __init__(self, core, send_sems, recv_sems):
-        self.core, self.send_sems, self.recv_sems, self.copies = core, send_sems, recv_sems, []
+        self.core, self.send_sems, self.recv_sems, self.copies, self.count = core, send_sems, recv_sems, [], 0
 
     def start(self, source, target, to):
-        i = len(self.copies)
+        i = self.count + len(self.copies)
         copy = pltpu.make_async_remote_copy(
             src_ref=source, dst_ref=target, send_sem=self.send_sems.at[i], recv_sem=self.recv_sems.at[i],
             device_id=to, device_id_type=MESH,
@@ -79,6 +79,7 @@
     def wait_sends(self):
         for copy in self.copies:
             copy.wait_send()
+        self.copies, self.count = [], self.count + len(self.copies)
 
 
 STEPS = (2, 1, 3)
@@ -165,9 +166,9 @@
 
 def step_kernel(
     loader_ref, ids_ref, nys_ref, eig_ref, scale_ref, centers_hbm, weights_hbm, labels_hbm,
-    new_hbm, res_hbm,
-    cent, wts, labs, pick, stack, kern, cand, mini, cnorm, ncol, mnorm, total, summed,
-    own_eig, got_eig, idcol, half_c, half_s, steps, partial, *rest,
+    base_hbm, res_hbm, coef_hbm, late_hbm, spread_hbm,
+    cent, wts, labs, pick, stack, kern, cand, mini, cnorm, turned, mnorm, total, summed,
+    own_eig, got_eig, idcol, half_c, half_s, partial, coef, *rest,
 ):
     bslots = [[rest[9 * u + 3 * s : 9 * u + 3 * s + 3] for s in range(3)] for u in range(2)]
     sslots = [[rest[18 + 9 * u + 3 * s : 21 + 9 * u + 3 * s] for s in range(3)] for u in range(2)]
@@ -221,7 +222,8 @@
     batch = [Reduction(links, bcast_index, BCAST_PARTS, cand, mini, bslots[u], chip, u * 2 + core) for u in range(2)]
     sums = [Reduction(links, sum_index, SUM_PARTS, total, summed, sslots[u], chip, u * 2 + core) for u in range(2)]
     eig_copies = []
-    pick_block(other)
+    for block in (other, core, 2 + other):
+        pick_block(block)
     for u in range(2):
         mine, theirs = u * 2 + core, u * 2 + other
         if u == 0:
@@ -237,10 +239,9 @@
                 to = device(to_chip, to_core)
                 eig_copies.append(links.start(own_eig.at[:, span(to[1], 128)], got_eig.at[my_nys], to))
             got_eig[my_nys] = own_eig[:, span(my_nys, 128)]
-        pick_block(mine)
+        if u == 1:
+            pick_block(mine)
         candidates(mine)
-        if u == 0:
-            pick_block(2 + other)
         first.wait_recv()
 
         def add_half(k, _):
@@ -249,18 +250,11 @@
 
         lax.fori_loop(0, 4, add_half, 0)
         batch[u].scatter_all()
-    def targets(x):
-        def put(k, _):
-            wanted = pick[span(k, 256), :]
-            if x < 3:
-                got = lax.dot_general(labs[pl.ds(x * 320, 320), :], wanted, NT, preferred_element_type=F32)
-            else:
-                got = lax.dot_general(labs[pl.ds(960, 40), :], wanted, NT, preferred_element_type=F32)
-                got = jnp.concatenate([got, jnp.zeros((280, 256), F32)], axis=0)
-            total[k, pl.ds(x * 320, 320), :] = got.astype(BF16)
-            return 0
-
-        lax.fori_loop(0, 4, put, 0)
+    def targets(quarter):
+        wanted = pick[pl.ds(quarter * 256, 256), :]
+        got = lax.dot_general(labs[...], wanted, NT, preferred_element_type=F32)
+        got = jnp.concatenate([got, jnp.zeros((ROWS - OUT, 256), F32)], axis=0)
+        total[quarter] = got.astype(BF16)
 
     def center_norms():
         def put(k, _):
@@ -302,18 +296,11 @@
         lax.fori_loop(0, 16, put, 0)
 
     def kernel_quarter(quarter, midway=None):
-        def rows_of(k, _):
-            block = mini[quarter, k].reshape(64, D)
-            norm = jnp.sum(jnp.square(block.astype(F32)), axis=1, keepdims=True)
-            ncol[span(k, 64), :] = jnp.broadcast_to(norm, (64, 128))
-            return 0
-
-        lax.fori_loop(0, 4, rows_of, 0)
-        mnorm[...] = ncol[...].T[0:8, :]
+        turned[...] = mini[quarter].reshape(256, D).T
+        mnorm[...] = jnp.broadcast_to(jnp.sum(jnp.square(turned[...].astype(F32)), axis=0, keepdims=True), (8, 256))
 
         def inner(k):
-            rows = mini[quarter].reshape(256, D)
-            return lax.dot_general(cent[pl.ds(k * 256, 256), :], rows, NT, preferred_element_type=F32)
+            return jnp.dot(cent[pl.ds(k * 256, 256), :], turned[...], preferred_element_type=F32)
 
         following = inner(0)
         for k in range(8):
@@ -367,8 +354,13 @@
         eigs = [summed[2 * u + h, pl.ds(EIG_ROW, Q), :] for h in range(2)]
         return lax.dot_general(residual_of(u), jnp.concatenate(eigs, axis=1), NT, preferred_element_type=F32)
 
-    def taken(u, k):
-        return jnp.dot(residual_of(u), pick[pl.ds(u * 512, 512), pl.ds(k * 512, 512)], preferred_element_type=F32)
+    def base_block(k):
+        columns = pl.ds(k * 512, 512)
+        taken = jnp.dot(residual_of(0), pick[pl.ds(0, 512), columns], preferred_element_type=F32)
+        wts[:, columns] = (wts[:, columns].astype(F32) - learn_rate * taken[:OUT]).astype(BF16)
+        out = pltpu.make_async_copy(wts.at[:, columns], base_hbm.at[:, columns], local_sems.at[7 + k])
+        out.start()
+        return out
 
     def residual_out(u):
         outs = []
@@ -381,7 +373,13 @@
 
     stack_rows()
     stack_tail()
+    early = [
+        pltpu.make_async_copy(idcol.at[pl.ds(512, 512), :], late_hbm, local_sems.at[12]),
+        pltpu.make_async_copy(stack.at[pl.ds(EIG_ROW, Q), :], spread_hbm, local_sems.at[13]),
+    ]
     loads[2].wait()
+    for out in early:
+        out.start()
     targets(0)
     for chunk in batch:
         chunk.second()
@@ -414,28 +412,31 @@
     sums[1].gather_second()
     first = sums[0].swap(sibling)
     first.wait_recv()
-    outs = residual_out(0)
-    for k in range(2):
-        steps[:, pl.ds(k * 512, 512)] = taken(0, k)
+    outs = residual_out(0) + early
+    outs += [base_block(k) for k in range(2)]
     sums[1].gather_first()
-    for k in range(2, 4):
-        steps[:, pl.ds(k * 512, 512)] = taken(0, k)
+    outs += [base_block(k) for k in range(2, 4)]
     partial[...] = reduced_of(0)
+    links.wait_sends()
     first = sums[1].swap(sibling)
     first.wait_recv()
     outs += residual_out(1)
-    coefficients = ((partial[...] + reduced_of(1)) * scale_ref[...]).astype(BF16)
-    for k in range(4):
-        columns = pl.ds(k * 512, 512)
-        step = jnp.dot(coefficients, stack[pl.ds(EIG_ROW, Q), columns], preferred_element_type=F32)
-        step -= steps[:, columns] + taken(1, k)
-        wts[:, columns] = (wts[:, columns].astype(F32) + learn_rate * step[:OUT]).astype(BF16)
-        out = pltpu.make_async_copy(wts.at[:, columns], new_hbm.at[:, columns], local_sems.at[7 + k])
-        out.start()
-        outs.append(out)
+    coef[...] = ((partial[...] + reduced_of(1)) * scale_ref[...])[:OUT].astype(BF16)
+    outs.append(pltpu.make_async_copy(coef, coef_hbm, local_sems.at[11]))
+    outs[-1].start()
     links.wait_sends()
     for out in outs:
         out.wait()
+
+
+def finish_kernel(base_ref, late_ref, part_ref, coef_ref, ids_ref, spread_ref, new_ref, res_ref):
+    ids = ids_ref[...].astype(jnp.int32) - pl.program_id(0) * 512
+    lane = lax.broadcasted_iota(jnp.int32, (512, 128), 1)
+    pick = jnp.concatenate([jnp.where(lane + j * 128 == ids, 1.0, 0.0).astype(BF16) for j in range(4)], axis=1)
+    step = jnp.dot(coef_ref[...], spread_ref[...], preferred_element_type=F32)
+    step -= jnp.dot(late_ref[...], pick, preferred_element_type=F32)
+    new_ref[...] = (base_ref[...].astype(F32) + learn_rate * step).astype(BF16)
+    res_ref[...] = part_ref[...]
 
 
 def body(centers, weights, labels, loader, sample_ids, nys_ids, eigen_vectors, eigen_scale):
@@ -450,7 +451,7 @@
         pltpu.VMEM((4, 4, 4, 16, D), BF16),
         pltpu.VMEM((4, 4, 4, 16, D), BF16),
         pltpu.VMEM((C_DEV, 128), F32),
-        pltpu.VMEM((256, 128), F32),
+        pltpu.VMEM((D, QUARTER), BF16),
         pltpu.VMEM((8, 256), F32),
         pltpu.VMEM((4, ROWS, QUARTER), BF16),
         pltpu.VMEM((4, ROWS, QUARTER), BF16),
@@ -459,22 +460,25 @@
         pltpu.VMEM((BATCH, 128), F32),
         pltpu.VMEM((2, 4, 4, 16, D), BF16),
         pltpu.VMEM((2, ROWS, QUARTER), BF16),
-        pltpu.VMEM((EIG_ROW, C_DEV), F32),
         pltpu.VMEM((EIG_ROW, Q), F32),
+        pltpu.VMEM((OUT, Q), BF16),
     ]
     for parts, shape in ((BCAST_PARTS, bcast_shape), (SUM_PARTS, sum_shape)):
         for stage in (0, 1, 2, 0, 1, 2):
             scratch += [pltpu.VMEM((3 + stage // 2,) + shape(part, stage), BF16) for part in parts]
     count = 3 + 2 * (1 + 45 + 1) + 2 * (12 + 45 + 1)
-    scratch += [pltpu.SemaphoreType.DMA((count,)), pltpu.SemaphoreType.DMA((count,)), pltpu.SemaphoreType.DMA((11,))]
-    new_weights, residual = pl.pallas_call(
+    scratch += [pltpu.SemaphoreType.DMA((count,)), pltpu.SemaphoreType.DMA((count,)), pltpu.SemaphoreType.DMA((14,))]
+    base, residual, coef, late_ids, spread = pl.pallas_call(
         step_kernel,
         out_shape=(
             jax.ShapeDtypeStruct((OUT, C_DEV), BF16),
             jax.ShapeDtypeStruct((OUT, BATCH), BF16),
+            jax.ShapeDtypeStruct((OUT, Q), BF16),
+            jax.ShapeDtypeStruct((512, 128), F32),
+            jax.ShapeDtypeStruct((Q, C_DEV), BF16),
         ),
         in_specs=[pl.BlockSpec(memory_space=pltpu.SMEM), vmem, vmem, vmem, vmem, anywhere, anywhere, anywhere],
-        out_specs=(anywhere, anywhere),
+        out_specs=(anywhere,) * 5,
         scratch_shapes=scratch,
         compiler_params=pltpu.CompilerParams(
             collective_id=0, has_side_effects=True, vmem_limit_bytes=62 * 2**20
@@ -484,6 +488,25 @@
         loader, sample_ids.reshape(1, BATCH), nys_ids.reshape(1, NYS_DEV), eigen_vectors.T, eigen_scale.reshape(1, Q),
         centers, weights.T, labels.T,
     )
+    new_weights, residual = pl.pallas_call(
+        finish_kernel,
+        out_shape=(
+            jax.ShapeDtypeStruct((OUT, C_DEV), BF16),
+            jax.ShapeDtypeStruct((OUT, BATCH), BF16),
+        ),
+        grid=(4,),
+        in_specs=[
+            pl.BlockSpec((OUT, 512), lambda i: (0, i)),
+            pl.BlockSpec((OUT, 512), lambda i: (0, 1)),
+            pl.BlockSpec((OUT, 256), lambda i: (0, i)),
+            pl.BlockSpec((OUT, Q), lambda i: (0, 0)),
+            pl.BlockSpec((512, 128), lambda i: (0, 0)),
+            pl.BlockSpec((Q, 512), lambda i: (0, i)),
+        ],
+        out_specs=(pl.BlockSpec((OUT, 512), lambda i: (0, i)), pl.BlockSpec((OUT, 256), lambda i: (0, i))),
+        compiler_params=pltpu.CompilerParams(vmem_limit_bytes=60 * 2**20),
+        name="finish",
+    )(base, residual, residual, coef, late_ids, spread)
     return (new_weights.T, residual.T)
 
 

time: 98.2 us -> 95.7 us (0.975)
  local copies, waits for them, and re-layouts: 6.15 us -> 0 us
  Pallas kernels: 90.6 us -> 94.1 us
    pallas_call x0 -> x1, Pallas kernels: none -> 8.37 us  [body(): pl.pallas_call(finish_kernel, out_shape=(jax.ShapeDtypeStruct((OUT, C_DEV...]
    unnamed x4 -> x0, local copies, waits for them, and re-layouts: 6.15 us -> none
    pallas_call x1, Pallas kernels: 90.6 us -> 85.7 us  [body(): pl.pallas_call(step_kernel, out_shape=(jax.ShapeDtypeStruct((OUT, C_DEV),...]
where the time goes in v3:
time: 95.7 us; the launch traced here: 95.4 us
  Pallas kernels  94.1 us (98%)
  between operations  1.29 us (1%)
    pallas_call x1, Pallas kernels, body(): pl.pallas_call(step_kernel, out_shape=(jax.ShapeDtypeStruct((OUT, C_DEV),...  85.7 us
    pallas_call x1, Pallas kernels, body(): pl.pallas_call(finish_kernel, out_shape=(jax.ShapeDtypeStruct((OUT, C_DEV...  8.37 us

profile of v3, /device:TPU:1, one launch (start us, length us, event | category | flops | bytes accessed | tf_op | source)
XLA Modules:
  0.0 95.4 jit_solution(16797190470350369571)
XLA Ops:
  1.3 85.7 %step.1 = (bf16[1000,2048]{1,0:T(8,128)(2,1)}, bf16[1000,1024]{1,0:T(8,128)(2,1)}, bf16[1000,160]{1,0:T(8,128)(2,1)}, f32[512,128]{1,0:T(8,128)}, bf16[160,2048]{1,0:T(8,128)(2,1)}) custom-call(s32[1]{0:T(128)S(6)} %copy.10.loader_ref, s32[1,1024]{1,0:T(1,128)} %bitcast.11, s32[1,128]{1,0:T(1,128)} %bitcast.13, bf16[40,512]{1,0:T(8,128)(2,1)} %bitcast.10, ...), custom_call_target="tpu_custom_call" | custom-call | tf_op jit(solution)/shard_map/step/pallas_call | solution.py:471
  87.0 8.4 %finish.1 = (bf16[1000,2048]{1,0:T(8,128)(2,1)}, bf16[1000,1024]{1,0:T(8,128)(2,1)}) custom-call(bf16[1000,2048]{1,0:T(8,128)(2,1)} %get-tuple-element.9.base_ref, bf16[1000,1024]{1,0:T(8,128)(2,1)} %get-tuple-element.10.late_ref.part_ref, bf16[1000,1024]{1,0:T(8,128)(2,1)} %get-tuple-element.10.late_ref.part_ref, ...), custom_call_target="tpu_custom_call" | custom-call | tf_op jit(solution)/shard_map/finish/pallas_call | solution.py:491

commit v4 on v3

--- a/solution.py
+++ b/solution.py
@@ -371,28 +371,28 @@
             outs[-1].start()
         return outs
 
+    loads[2].wait()
+    targets(0)
+    targets(1)
+    for chunk in batch:
+        chunk.second()
+    targets(2)
+    for chunk in batch:
+        chunk.exchange()
+    targets(3)
+    for chunk in batch:
+        chunk.gather_second()
+    center_norms()
+    for chunk in batch:
+        chunk.gather_first()
     stack_rows()
     stack_tail()
     early = [
         pltpu.make_async_copy(idcol.at[pl.ds(512, 512), :], late_hbm, local_sems.at[12]),
         pltpu.make_async_copy(stack.at[pl.ds(EIG_ROW, Q), :], spread_hbm, local_sems.at[13]),
     ]
-    loads[2].wait()
     for out in early:
         out.start()
-    targets(0)
-    for chunk in batch:
-        chunk.second()
-    targets(1)
-    for chunk in batch:
-        chunk.exchange()
-    targets(2)
-    for chunk in batch:
-        chunk.gather_second()
-    targets(3)
-    for chunk in batch:
-        chunk.gather_first()
-    center_norms()
     swaps = [batch[0].swap(sibling)]
     kernel_quarter(core)
     swaps[0].wait_recv()
@@ -407,8 +407,8 @@
     own_products(1, copies)
     sums[0].gather_second()
     sums[1].second()
+    sums[1].exchange()
     sums[0].gather_first()
-    sums[1].exchange()
     sums[1].gather_second()
     first = sums[0].swap(sibling)
     first.wait_recv()

time: 95.7 us -> 95.1 us (level)
  no operation moved by 1% of the time
where the time goes in v4:
time: 95.1 us; the launch traced here: 94.8 us
  Pallas kernels  93.5 us (98%)
  between operations  1.29 us (1%)
    pallas_call x1, Pallas kernels, body(): pl.pallas_call(step_kernel, out_shape=(jax.ShapeDtypeStruct((OUT, C_DEV),...  85.1 us
    pallas_call x1, Pallas kernels, body(): pl.pallas_call(finish_kernel, out_shape=(jax.ShapeDtypeStruct((OUT, C_DEV...  8.37 us

profile of v4, /device:TPU:1, one launch (start us, length us, event | category | flops | bytes accessed | tf_op | source)
XLA Modules:
  0.0 94.8 jit_solution(3823170500237112816)
XLA Ops:
  1.3 85.1 %step.1 = (bf16[1000,2048]{1,0:T(8,128)(2,1)}, bf16[1000,1024]{1,0:T(8,128)(2,1)}, bf16[1000,160]{1,0:T(8,128)(2,1)}, f32[512,128]{1,0:T(8,128)}, bf16[160,2048]{1,0:T(8,128)(2,1)}) custom-call(s32[1]{0:T(128)S(6)} %copy.10.loader_ref, s32[1,1024]{1,0:T(1,128)} %bitcast.11, s32[1,128]{1,0:T(1,128)} %bitcast.13, bf16[40,512]{1,0:T(8,128)(2,1)} %bitcast.10, ...), custom_call_target="tpu_custom_call" | custom-call | tf_op jit(solution)/shard_map/step/pallas_call | solution.py:471
  86.4 8.4 %finish.1 = (bf16[1000,2048]{1,0:T(8,128)(2,1)}, bf16[1000,1024]{1,0:T(8,128)(2,1)}) custom-call(bf16[1000,2048]{1,0:T(8,128)(2,1)} %get-tuple-element.9.base_ref, bf16[1000,1024]{1,0:T(8,128)(2,1)} %get-tuple-element.10.late_ref.part_ref, bf16[1000,1024]{1,0:T(8,128)(2,1)} %get-tuple-element.10.late_ref.part_ref, ...), custom_call_target="tpu_custom_call" | custom-call | tf_op jit(solution)/shard_map/finish/pallas_call | solution.py:491
